TPU v7x, 512 devices: a whole 4x8x8 slice. The times are simulated.
512 devices in a mesh: dp: 512 (over y, z, x, core).
Axes of the slice: x: 4, y: 8, z: 8, core: 2. Of those that a mesh axis runs over, the one named last changes fastest.
Arguments:
- entry_input: bfloat16 [65536, 3072], P('dp'), may hold values from -6 to 6
- entry_grad: bfloat16 [65536, 6144], P('dp'), may hold values from -6 to 6
- exit_input: bfloat16 [65536, 4096], P('dp'), may hold values from -6 to 6
- exit_grad: bfloat16 [65536, 3072], P('dp'), may hold values from -6 to 6
- entry_left: bfloat16 [8192, 3072], P('dp'), may hold values from -6 to 6
- entry_right: bfloat16 [8192, 6144], P('dp'), may hold values from -6 to 6
- exit_left: bfloat16 [8192, 4096], P('dp'), may hold values from -6 to 6
- exit_right: bfloat16 [8192, 3072], P('dp'), may hold values from -6 to 6
- entry_start: float32 [6144, 32], P('dp'), may hold values from -6 to 6
- exit_start: float32 [3072, 32], P('dp'), may hold values from -6 to 6
Outputs:
- entry_basis: float32 [3072, 32], P('dp')
- exit_basis: float32 [4096, 32], P('dp')
- entry_factor: float32 [6144, 32], P('dp')
- exit_factor: float32 [3072, 32], P('dp')
All inputs are finite; a program needn't handle non-finite values.
Results may differ from a plain program's by a relative error of at most 0.0003.
Values sent between devices are 32-bit elements; how exact they have to be, the bound alone decides.
A program may use at most 64 MiB of HBM per device.

v0:
```python
import math

import jax
import jax.numpy as jnp
from jax import lax
from jax.sharding import PartitionSpec as P


def product(a, b):
    return jnp.dot(a, b, precision=lax.Precision.HIGHEST, preferred_element_type=jnp.float32)


def orthonormal(rows_block, gram):
    lower = jnp.linalg.cholesky(gram)
    return jax.scipy.linalg.solve_triangular(lower, rows_block.T, lower=True).T


def left_local(inputs, grads, left_rows, right_rows, start):
    return product(inputs.T, product(grads, start)) + product(
        left_rows.T, product(right_rows, start)
    )


def right_local(inputs, grads, left_rows, right_rows, basis):
    return product(grads.T, product(inputs, basis)) + product(
        right_rows.T, product(left_rows, basis)
    )


def own_rows(whole, replicas, position):
    share_rows = whole.shape[0] // replicas
    return lax.dynamic_slice_in_dim(whole, position * share_rows, share_rows, 0)


def body(
    entry_input,
    entry_grad,
    exit_input,
    exit_grad,
    entry_left,
    entry_right,
    exit_left,
    exit_right,
    entry_start,
    exit_start,
):
    replicas = lax.axis_size("dp")
    position = lax.axis_index("dp")
    start_entry, start_exit = (
        lax.all_gather(entry_start, "dp", axis=0, tiled=True),
        lax.all_gather(exit_start, "dp", axis=0, tiled=True),
    )
    local_entry = left_local(entry_input, entry_grad, entry_left, entry_right, start_entry)
    local_exit = left_local(exit_input, exit_grad, exit_left, exit_right, start_exit)
    summed_entry, summed_exit = lax.psum((local_entry, local_exit), "dp")
    basis_entry = orthonormal(summed_entry, product(summed_entry.T, summed_entry))
    basis_exit = orthonormal(summed_exit, product(summed_exit.T, summed_exit))
    own_entry = own_rows(basis_entry, replicas, position)
    own_exit = own_rows(basis_exit, replicas, position)
    right_entry = right_local(entry_input, entry_grad, entry_left, entry_right, basis_entry)
    right_exit = right_local(exit_input, exit_grad, exit_left, exit_right, basis_exit)
    whole_entry, whole_exit = lax.psum((right_entry, right_exit), "dp")
    part_entry = own_rows(whole_entry, replicas, position)
    part_exit = own_rows(whole_exit, replicas, position)
    entry_width = entry_input.shape[1]
    exit_width = exit_input.shape[1]
    return (
        own_entry * math.sqrt(entry_width),
        own_exit * math.sqrt(exit_width),
        part_entry / replicas,
        part_exit / replicas,
    )


def solution(mesh):
    in_specs = (
        P("dp", None),
        P("dp", None),
        P("dp", None),
        P("dp", None),
        P("dp", None),
        P("dp", None),
        P("dp", None),
        P("dp", None),
        P("dp", None),
        P("dp", None),
    )
    out_specs = (P("dp", None), P("dp", None), P("dp", None), P("dp", None))
    return jax.shard_map(body, mesh=mesh, in_specs=in_specs, out_specs=out_specs, check_vma=False)
```

profile of v0, /device:TPU:1, one launch (start us, length us, event | category | flops | bytes accessed | tf_op | source)
XLA Modules:
  0.0 764.7 jit_solution(401959426592411661)
XLA Ops:
  7.2 0.0 copy-start
  7.2 0.0 all-reduce.7.cloned.1.call-start
  7.2 92.0 %all-gather = f32[512,12,32]{2,1,0:T(8,128)} all-gather(f32[1,12,32]{2,1,0:T(8,128)} %bitcast.70), channel_id=1, replica_groups=mesh['dp'=512] {'dp'}, dimensions={0}, use_global_device_ids=true | all-gather | bytes 787968 | tf_op jit(solution)/shard_map/all_gather | solution.py:50
  99.2 4.6 reshape.22
  103.8 0.0 copy-done
  103.8 4.6 fusion.12
  108.5 0.0 copy-done.1
  108.5 0.0 copy-done.6
  108.5 0.0 copy-start.10
  108.5 1.1 fusion.14
  109.6 0.0 copy-done.10
  109.6 72.8 %all-gather.1 = f32[512,6,32]{2,1,0:T(8,128)} all-gather(f32[1,6,32]{2,1,0:T(8,128)S(1)} %bitcast.71), channel_id=1, replica_groups=mesh['dp'=512] {'dp'}, dimensions={0}, use_global_device_ids=true | all-gather | bytes 393984 | tf_op jit(solution)/shard_map/all_gather | solution.py:51
  182.4 1.6 reshape.24
  184.0 0.0 copy-start.8
  184.0 0.0 copy-start.4
  184.1 2.6 fusion.16
  186.6 0.0 copy-done.8
  186.6 0.0 copy-start.3
  186.6 0.6 fusion.18
  187.3 0.0 copy-done.4
  187.3 0.0 copy-start.9
  187.3 0.0 copy-start.7
  187.3 0.4 fusion.13
  187.7 0.1 copy-done.3
  187.9 0.5 fusion.17
  188.4 1.1 fusion.3
  189.5 1.2 fusion.1
  190.7 0.0 all-reduce.7.cloned.1.call-update
  190.7 0.3 all-reduce.5.cloned.1.call-start
  191.0 266.9 %all-reduce.7.cloned.1.call-done = (f32[3072,32]{0,1:T(8,128)}, f32[4096,32]{0,1:T(8,128)}) async-done(((f32[3072,32]{0,1:T(8,128)}, f32[4096,32]{0,1:T(8,128)}), (f32[3072,32]{0,1:T(8,128)}, f32[4096,32]{0,1:T(8,128)})) %all-reduce.7.cloned.1.call-update) | async-done | bytes 917520 | tf_op jit(solution)/shard_map/psum | solution.py:55
  457.9 1.6 fusion.15
  459.5 0.1 copy.26
  459.6 2.9 cholesky.44
  462.6 0.6 compare_reduce_fusion.1
  463.2 0.7 fusion.4
  463.9 2.4 custom-call.10
  466.3 1.5 fusion.9
  467.9 2.0 fusion.20
  469.8 0.3 fusion.22
  470.1 0.6 fusion.19
  470.7 0.1 copy.27
  470.8 2.9 cholesky.55
  473.7 0.6 compare_reduce_fusion
  474.4 0.7 fusion.5
  475.1 2.4 custom-call.11
  477.5 0.7 fusion.6
  478.1 2.3 fusion.23
  480.4 0.0 copy-start.5
  480.5 0.4 fusion.25
  480.8 0.8 fusion.21
  481.6 0.0 copy-done.5
  481.6 0.4 fusion.24
  482.0 1.4 fusion
  483.4 1.1 fusion.2
  484.6 0.0 all-reduce.5.cloned.1.call-update
  484.6 0.1 multiply_bitcast_fusion.1
  484.7 0.7 copy.28
  485.3 0.1 multiply_bitcast_fusion
  485.4 0.7 copy.29
  486.1 268.8 %all-reduce.5.cloned.1.call-done = (f32[6144,32]{0,1:T(8,128)}, f32[3072,32]{0,1:T(8,128)}) async-done(((f32[6144,32]{0,1:T(8,128)}, f32[3072,32]{0,1:T(8,128)}), (f32[6144,32]{0,1:T(8,128)}, f32[3072,32]{0,1:T(8,128)})) %all-reduce.5.cloned.1.call-update) | async-done | bytes 1179664 | tf_op jit(solution)/shard_map/psum | solution.py:62
  754.9 0.8 dynamic-slice_multiply_fusion.1
  755.7 0.7 copy.30
  756.4 0.8 dynamic-slice_multiply_fusion
  757.2 0.7 copy.31
  (10 shorter events, 0.1 us)
Async XLA Ops:
  7.2 96.7 %copy-start = (bf16[128,6144]{1,0:T(8,128)(2,1)S(1)}, bf16[128,6144]{1,0:T(8,128)(2,1)}, u32[]{:S(2)}) copy-start(bf16[128,6144]{1,0:T(8,128)(2,1)} %param.12) | copy-start | bytes 4718596
  7.2 450.7 %all-reduce.7.cloned.1.call-start = ((), (), s32[]{:S(2)}) async-start(), calls=%async_computation.1 | async-start | bytes 1835008 | tf_op jit(solution)/shard_map/psum | solution.py:55
  103.8 4.6 copy-start.1
  103.8 4.6 copy-start.6
  108.5 1.1 copy-start.10
  184.0 2.6 copy-start.8
  184.0 3.2 copy-start.4
  186.6 1.2 copy-start.3
  187.3 1.1 copy-start.9
  187.3 2.2 copy-start.7
  190.7 564.1 %all-reduce.5.cloned.1.call-start = ((), (), s32[]{:S(2)}) async-start(), calls=%async_computation | async-start | bytes 2359296 | tf_op jit(solution)/shard_map/psum | solution.py:62
  457.9 12.2 %copy-start.2 = (f32[4096,32]{0,1:T(8,128)S(1)}, f32[4096,32]{0,1:T(8,128)}, u32[]{:S(2)}) copy-start(f32[4096,32]{0,1:T(8,128)} %get-tuple-element.20) | copy-start | bytes 1572868
  480.4 1.2 copy-start.5
Sparse Core Ops, SparseCore 0:
  190.9 267.0 all-reduce.6
  484.7 270.1 all-reduce.4
where the time goes:
time: 765 us
  waiting for transfers between devices  536 us (70%)
  blocking collectives  165 us (22%)
  matrix products  25.2 us (3%)
  other arithmetic  15.2 us (2%)
  between operations  14.2 us (2%)
  local copies, waits for them, and re-layouts  9.25 us (1%)
    psum x1, waiting for transfers between devices, body(): whole_entry, whole_exit = lax.psum((right_entry, right_exit), 'dp')  269 us
    psum x1, waiting for transfers between devices, body(): summed_entry, summed_exit = lax.psum((local_entry, local_exit), 'dp')  267 us
    all_gather x1, blocking collectives, body(): lax.all_gather(entry_start, 'dp', axis=0, tiled=True)  92 us
    all_gather x1, blocking collectives, body(): lax.all_gather(exit_start, 'dp', axis=0, tiled=True)  72.8 us
    dot_general x18, matrix products, product(): jnp.dot(a, b, precision=lax.Precision.HIGHEST, preferred_element_type=jnp...  23.1 us
  transfers between devices with their start and end apart: 2, of which 2 were waited for; matrix products, arithmetic and copies ran while one was open for 0% of the time, Pallas kernels for 0%

commit v1 on v0

v1 whole, which is shorter than its diff:
```python
import functools
import math

import jax
import jax.numpy as jnp
from jax import lax
from jax.experimental import pallas as pl
from jax.experimental.pallas import tpu as pltpu
from jax.sharding import PartitionSpec as P

MESH = pl.DeviceIdType.MESH
NY, NZ, NX = 8, 8, 4
GROUPS = 4
HALF = 4
TOK = 144
NS = 9
NL = 7
F32 = jnp.float32
BF16 = jnp.bfloat16
NT = (((1,), (1,)), ((), ()))
NN = (((1,), (0,)), ((), ()))
TN = (((0,), (0,)), ((), ()))


def device(y, z, x, c):
    return ((y * NZ + z) * NX + x) * 2 + c


def split3(v):
    hi = v.astype(BF16)
    rest = v - hi.astype(F32)
    mid = rest.astype(BF16)
    lo = (rest - mid.astype(F32)).astype(BF16)
    return jnp.concatenate([hi, mid, lo], axis=0)


def fold3(v):
    return v[0:32] + v[32:64] + v[64:96]


def exact_dot(a, b, dims):
    return lax.dot_general(a, b, dims, precision=lax.Precision.HIGHEST, preferred_element_type=F32)


def entry_window(z):
    return 3 * (z // 4) + (z % 4) // 2


def exit_window(z):
    return z // 4


def iota(shape, dim):
    return lax.broadcasted_iota(jnp.int32, shape, dim)


def kernel(
    entry_input, entry_grad, exit_input, exit_grad,
    entry_left, entry_right, exit_left, exit_right,
    entry_start, exit_start,
    out,
    wxe, wge, wxx, wgx, own_start,
    s_all, l_all,
    first_send, first_recv, zs_send, zs_recv,
    l_loc, l_core, l_x, l_ys, l_y, l_zs, l_z,
    f_loc, f_core, f_x, f_ys, f_y, f_zs, f_z, f_last, f_own,
    load_sem,
    first_ss, first_rs, zs_ss, zs_rs, lz_ss, lz_rs, fz_ss, fz_rs, last_ss, last_rs,
    sg_ys, sg_yr, sg_xs, sg_xr, sg_cs, sg_cr,
    lg_ys, lg_yr, lg_xs, lg_xr, lg_cs, lg_cr,
    lr_cs, lr_cr, lr_xs, lr_xr, lr_ys, lr_yr,
    fr_cs, fr_cr, fr_xs, fr_xr, fr_ys, fr_yr,
):
    me = lax.axis_index("dp")
    y, z, x, c = me // (NZ * NX * 2), (me // (NX * 2)) % NZ, (me // 2) % NX, me % 2
    active_core = y // HALF
    active = c == active_core
    other = device(y, z, x, 1 - c)
    spot = 2 * x + c
    pending = []

    def remote(src, dst, ss, rs, target):
        return pltpu.make_async_remote_copy(
            src_ref=src, dst_ref=dst, send_sem=ss, recv_sem=rs, device_id=(target,), device_id_type=MESH
        )

    def guarded(cond, fn):
        if cond is None:
            fn()
        else:
            @pl.when(cond)
            def _():
                fn()

    def send(src, dst, ss, rs, target, cond=None):
        copy = remote(src, dst, ss, rs, target)
        guarded(cond, copy.start)
        pending.append((cond, copy))

    def arrive(dst, ss, rs, cond=None):
        copy = remote(dst, dst, ss, rs, other)
        guarded(cond, copy.wait_recv)

    loads = []
    for i, (src, dst, row, rows) in enumerate((
        (entry_grad, wge, 0, 128), (entry_right, wge, 128, 16),
        (exit_grad, wgx, 0, 128), (exit_right, wgx, 128, 16),
        (entry_input, wxe, 0, 128), (entry_left, wxe, 128, 16),
        (exit_input, wxx, 0, 128), (exit_left, wxx, 128, 16),
    )):
        copy = pltpu.make_async_copy(src, dst.at[pl.ds(row, rows)], load_sem.at[i])
        copy.start()
        loads.append(copy)

    barrier = pltpu.get_barrier_semaphore()
    peers = [device(y, z, (x + k // 2) % NX, (c + k) % 2) for k in range(1, 8)]
    peers += [device(y, (z + k) % NZ, x, c) for k in range(1, 8)]
    peers += [device((y + k) % NY, z, x, c) for k in range(1, 8)]
    for peer in peers:
        pl.semaphore_signal(barrier, inc=1, device_id=(peer,), device_id_type=MESH)

    own_start[...] = jnp.zeros_like(own_start)
    own_start[0:12, :] = entry_start[...]
    own_start[16:22, :] = exit_start[...]
    at_entry = 96 * z - 128 * entry_window(z) + 12 * spot
    at_exit = 48 * z - 128 * exit_window(z) + 6 * spot
    pick_entry = jnp.where(
        (iota((16, 256), 1) == at_entry + iota((16, 256), 0)) & (iota((16, 256), 0) < 12), 1.0, 0.0
    ).astype(F32)
    pick_exit = jnp.where(
        (iota((16, 256), 1) == at_exit + iota((16, 256), 0)) & (iota((16, 256), 0) < 6), 1.0, 0.0
    ).astype(F32)
    placed_entry = exact_dot(own_start[0:16, :], pick_entry, TN)
    placed_exit = exact_dot(own_start[16:32, :], pick_exit, TN)
    for g in range(GROUPS):
        for t in range(2):
            first_send[g, t] = placed_entry[8 * g:8 * g + 8, 128 * t:128 * t + 128]
            first_send[g, 2 + t] = placed_exit[8 * g:8 * g + 8, 128 * t:128 * t + 128]

    pl.semaphore_wait(barrier, len(peers))

    send(first_send.at[x], first_recv.at[spot], first_ss.at[0], first_rs.at[spot], other, jnp.logical_not(active))
    for k in range(1, 4):
        to = (x + k) % NX
        send(first_send.at[to], first_recv.at[spot], first_ss.at[k], first_rs.at[spot], device(y, z, to, active_core))

    @pl.when(active)
    def _():
        total = [first_send[x, t] for t in range(4)]
        for k in range(1, 8):
            source = (spot + k) % 8
            arrive(first_recv.at[source], first_ss.at[0], first_rs.at[source])
            for t in range(4):
                total[t] = total[t] + first_recv[source, t]
        for t in range(4):
            zs_send[t] = total[t]

    for k in range(1, 8):
        send(zs_send, zs_recv.at[z], zs_ss.at[k], zs_rs.at[z], device(y, (z + k) % NZ, x, c), active)

    @pl.when(active)
    def _():
        for t in range(4):
            zs_recv[z, t] = zs_send[t]
        for k in range(1, 8):
            source = (z + k) % NZ
            arrive(zs_recv.at[source], zs_ss.at[0], zs_rs.at[source])
        slab = [None] * NS
        for zz in range(NZ):
            for t in range(2):
                for at, tile in ((entry_window(zz) + t, zs_recv[zz, t]), (6 + exit_window(zz) + t, zs_recv[zz, 2 + t])):
                    slab[at] = tile if slab[at] is None else slab[at] + tile
        for t in range(NS):
            s_all[x, y * NS + t] = slab[t]

    def gather(whole, n, ys, yr, xs, xr, cs, cr, use):
        def part(group, slab):
            return whole.at[group, pl.ds(slab * n, n)]

        def full(slab):
            return whole.at[:, pl.ds(slab * n, n)]

        for k in range(1, 8):
            send(part(x, y), part(x, y), ys.at[k], yr.at[y], device((y + k) % NY, z, x, c), active)
        for j in range(HALF):
            at = (y + j) % HALF
            slab = HALF * c + at
            arrive(part(x, slab), ys.at[0], yr.at[slab], slab != y)
            for k in range(1, 4):
                send(part(x, slab), part(x, slab), xs.at[j, k], xr.at[at, x], device(y, z, (x + k) % NX, c))
        for j in range(HALF):
            at = (y + j) % HALF
            slab = HALF * c + at
            for k in range(1, 4):
                source = (x + k) % NX
                arrive(part(source, slab), xs.at[0, 0], xr.at[at, source])
            send(full(slab), full(slab), cs.at[j], cr.at[at], other)
            use(slab)
        for j in range(HALF):
            at = (y + j) % HALF
            slab = HALF * (1 - c) + at
            arrive(full(slab), cs.at[0], cr.at[at])
            use(slab)

    def reduce(n, produce, between, local, from_core, from_x, y_send, from_y, cs, cr, xs, xr, ys, yr, result):
        for j in range(HALF):
            slab = HALF * (1 - c) + j
            produce(slab)
            send(local.at[:, pl.ds(slab * n, n)], from_core.at[:, pl.ds(j * n, n)], cs.at[j], cr.at[j], other)
        for j in range(HALF):
            slab = HALF * c + j
            produce(slab)
            arrive(from_core.at[:, pl.ds(j * n, n)], cs.at[0], cr.at[j])
            for g in range(GROUPS):
                for t in range(n):
                    local[g, slab * n + t] = local[g, slab * n + t] + from_core[g, j * n + t]
            for k in range(1, 4):
                to = (x + k) % NX
                send(
                    local.at[to, pl.ds(slab * n, n)], from_x.at[x, pl.ds(j * n, n)], xs.at[j, k], xr.at[j, x],
                    device(y, z, to, c),
                )
        between()
        for j in range(HALF):
            slab = HALF * c + j
            total = [local[x, slab * n + t] for t in range(n)]
            for k in range(1, 4):
                source = (x + k) % NX
                arrive(from_x.at[source, pl.ds(j * n, n)], xs.at[0, 0], xr.at[j, source])
                for t in range(n):
                    total[t] = total[t] + from_x[source, j * n + t]
            for t in range(n):
                y_send[j, t] = total[t]
            send(y_send.at[j], from_y.at[y], ys.at[j], yr.at[y], device(slab, z, x, c), slab != y)

        @pl.when(active)
        def _():
            total = [y_send[y % HALF, t] for t in range(n)]
            for k in range(1, 8):
                source = (y + k) % NY
                arrive(from_y.at[source], ys.at[0], yr.at[source])
                for t in range(n):
                    total[t] = total[t] + from_y[source, t]
            result(total)

    def tiles(whole, first, count):
        return jnp.concatenate(
            [jnp.concatenate([whole[g, first + t] for t in range(count)], axis=1) for g in range(GROUPS)], axis=0
        )

    def lanes(ref, slab, width):
        return ref[:, pl.ds(pl.multiple_of(slab * width, 128), width)]

    def contract(whole, first, count, weights, slab):
        pieces = split3(tiles(whole, first, count))
        part = lax.dot_general(pieces, lanes(weights, slab, 128 * count), NT, preferred_element_type=F32)
        return fold3(part), pieces

    def expand(pieces, weights, slab, count, whole, first):
        part = fold3(lax.dot_general(pieces, lanes(weights, slab, 128 * count), NN, preferred_element_type=F32))
        for g in range(GROUPS):
            for t in range(count):
                whole[g, first + t] = part[8 * g:8 * g + 8, 128 * t:128 * t + 128]

    for copy in loads:
        copy.wait()

    sums = {"entry": jnp.zeros((32, TOK), F32), "exit": jnp.zeros((32, TOK), F32)}

    def use_start(slab):
        sums["entry"] += contract(s_all, slab * NS, 6, wge, slab)[0]
        sums["exit"] += contract(s_all, slab * NS + 6, 3, wgx, slab)[0]

    gather(s_all, NS, sg_ys, sg_yr, sg_xs, sg_xr, sg_cs, sg_cr, use_start)
    left_entry, left_exit = split3(sums["entry"]), split3(sums["exit"])

    def produce_left(slab):
        expand(left_entry, wxe, slab, 3, l_loc, slab * NL)
        expand(left_exit, wxx, slab, 4, l_loc, slab * NL + 3)

    def left_result(total):
        for t in range(NL):
            l_zs[t] = total[t]

    reduce(
        NL, produce_left, lambda: None, l_loc, l_core, l_x, l_ys, l_y,
        lr_cs, lr_cr, lr_xs, lr_xr, lr_ys, lr_yr, left_result,
    )
    for k in range(1, 8):
        send(l_zs, l_z.at[z], lz_ss.at[k], lz_rs.at[z], device(y, (z + k) % NZ, x, c), active)

    @pl.when(active)
    def _():
        for t in range(NL):
            l_z[z, t] = l_zs[t]
        for k in range(1, 8):
            source = (z + k) % NZ
            arrive(l_z.at[source], lz_ss.at[0], lz_rs.at[source])
        for t in range(NL):
            total = l_z[0, t]
            for zz in range(1, NZ):
                total = total + l_z[zz, t]
            l_all[x, y * NL + t] = total

    sides = {"entry": jnp.zeros((32, TOK), F32), "exit": jnp.zeros((32, TOK), F32)}
    grams = {"entry": jnp.zeros((32, 96), F32), "exit": jnp.zeros((32, 96), F32)}

    def use_left(slab):
        for name, first, count, weights in (("entry", 0, 3, wxe), ("exit", 3, 4, wxx)):
            part, pieces = contract(l_all, slab * NL + first, count, weights, slab)
            sides[name] += part
            grams[name] += fold3(lax.dot_general(pieces, pieces, NT, preferred_element_type=F32))

    gather(l_all, NL, lg_ys, lg_yr, lg_xs, lg_xr, lg_cs, lg_cr, use_left)
    right_entry, right_exit = split3(sides["entry"]), split3(sides["exit"])

    def produce_right(slab):
        expand(right_entry, wge, slab, 6, f_loc, slab * NS)
        expand(right_exit, wgx, slab, 3, f_loc, slab * NS + 6)

    inverse = {}

    def cholesky():
        row, column = iota((32, 32), 0), iota((32, 32), 1)
        state = {}
        for name in ("entry", "exit"):
            gram = grams[name]
            state[name] = [
                gram[:, 0:32] + gram[:, 32:64] + gram[:, 64:96],
                jnp.where(row == column, 1.0, 0.0).astype(F32),
                jnp.ones((32, 1), F32),
            ]
        rows = iota((32, 1), 0)
        for j in range(32):
            for name in ("entry", "exit"):
                left, unit, diagonal = state[name]
                pivot = left[j:j + 1, j:j + 1]
                factor = jnp.where(rows > j, left[:, j:j + 1] / pivot, 0.0)
                state[name] = [
                    left - factor * left[j:j + 1, :],
                    unit - factor * unit[j:j + 1, :],
                    jnp.where(rows == j, pivot, diagonal),
                ]
        for name in ("entry", "exit"):
            inverse[name] = state[name][1] / jnp.sqrt(state[name][2])
        for name, first, count, each, put, width in (("entry", 0, 3, 6, 0, 3072), ("exit", 3, 4, 8, 8, 4096)):
            shape = (8, 128 * count)
            at = each * (8 * z + spot)
            pick = jnp.where((iota(shape, 1) == at + iota(shape, 0)) & (iota(shape, 0) < each), 1.0, 0.0).astype(F32)
            own = exact_dot(pick, tiles(l_all, y * NL + first, count), NT)
            out[put:put + 8, :] = exact_dot(own, inverse[name], NT) * math.sqrt(width)

    def right_result(total):
        for zz in range(NZ):
            for t in range(2):
                f_zs[zz, t] = total[entry_window(zz) + t]
                f_zs[zz, 2 + t] = total[6 + exit_window(zz) + t]

    reduce(
        NS, produce_right, cholesky, f_loc, f_core, f_x, f_ys, f_y,
        fr_cs, fr_cr, fr_xs, fr_xr, fr_ys, fr_yr, right_result,
    )
    for k in range(1, 8):
        to = (z + k) % NZ
        send(f_zs.at[to], f_z.at[z], fz_ss.at[k], fz_rs.at[z], device(y, to, x, c), active)

    @pl.when(active)
    def _():
        total = [f_zs[z, t] for t in range(4)]
        for k in range(1, 8):
            source = (z + k) % NZ
            arrive(f_z.at[source], fz_ss.at[0], fz_rs.at[source])
            for t in range(4):
                total[t] = total[t] + f_z[source, t]
        for t in range(4):
            f_own[t] = total[t]

    for k in range(1, 8):
        send(
            f_own, f_last.at[x], last_ss.at[k], last_rs.at[x],
            device(y, z, (x + k // 2) % NX, (c + k) % 2), active,
        )

    @pl.when(active)
    def _():
        for t in range(4):
            f_last[x, t] = f_own[t]

    for k in range(4):
        source = (x + k) % NX
        arrive(f_last.at[source], last_ss.at[0], last_rs.at[source], jnp.logical_not(active) if k == 0 else None)
    for name, first, pick, put in (("entry", 0, pick_entry, 16), ("exit", 2, pick_exit, 32)):
        own = exact_dot(pick, tiles(f_last, first, 2), NT)
        out[put:put + 16, :] = exact_dot(own, inverse[name], NT) * (1.0 / 512)

    for cond, copy in pending:
        guarded(cond, copy.wait_send)


def outputs_kernel(packed, entry_basis, exit_basis, entry_factor, exit_factor):
    entry_basis[...] = packed[0:6, :]
    exit_basis[...] = packed[8:16, :]
    entry_factor[...] = packed[16:28, :]
    exit_factor[...] = packed[32:38, :]


def body(*args):
    dma = pltpu.SemaphoreType.DMA
    tile = (8, 128)

    def f32(*shape):
        return pltpu.VMEM(shape + tile, F32)

    def reduce_buffers(n):
        return [f32(4, 8 * n), f32(4, 4 * n), f32(4, 4 * n), f32(4, n), f32(8, n)]

    scratch = [
        pltpu.VMEM((TOK, 3072), BF16), pltpu.VMEM((TOK, 6144), BF16),
        pltpu.VMEM((TOK, 4096), BF16), pltpu.VMEM((TOK, 3072), BF16),
        pltpu.VMEM((32, 32), F32),
        f32(4, 8 * NS), f32(4, 8 * NL),
        f32(4, 4), f32(8, 4), f32(4), f32(8, 4),
        *reduce_buffers(NL), f32(NL), f32(8, NL),
        *reduce_buffers(NS), f32(8, 4), f32(8, 4), f32(4, 4), f32(4),
        dma((8,)),
        dma((4,)), dma((8,)), dma((8,)), dma((8,)), dma((8,)), dma((8,)), dma((8,)), dma((8,)), dma((8,)), dma((4,)),
    ]
    for _ in range(2):
        scratch += [dma((8,)), dma((8,)), dma((4, 4)), dma((4, 4)), dma((4,)), dma((4,))]
    for _ in range(2):
        scratch += [dma((4,)), dma((4,)), dma((4, 4)), dma((4, 4)), dma((4,)), dma((8,))]
    vmem = pl.BlockSpec(memory_space=pltpu.VMEM)
    anywhere = pl.BlockSpec(memory_space=pltpu.HBM)
    packed = pl.pallas_call(
        kernel,
        out_shape=jax.ShapeDtypeStruct((48, 32), F32),
        in_specs=[anywhere] * 8 + [vmem] * 2,
        out_specs=vmem,
        scratch_shapes=scratch,
        compiler_params=pltpu.CompilerParams(
            collective_id=0, has_side_effects=True, vmem_limit_bytes=48 * 1024 * 1024
        ),
        name="powersgd",
    )(*args)
    return pl.pallas_call(
        outputs_kernel,
        out_shape=tuple(jax.ShapeDtypeStruct((rows, 32), F32) for rows in (6, 8, 12, 6)),
        in_specs=[vmem],
        out_specs=(vmem,) * 4,
        name="outputs",
    )(packed)


def solution(mesh):
    spec = P("dp", None)
    return jax.shard_map(body, mesh=mesh, in_specs=(spec,) * 10, out_specs=(spec,) * 4, check_vma=False)
```

time: 765 us -> 111 us (0.15)
  waiting for transfers between devices: 536 us -> 0 us
  blocking collectives: 165 us -> 0 us
  Pallas kernels: 0 us -> 98.8 us
  matrix products: 25.2 us -> 0 us
  other arithmetic: 15.2 us -> 0 us
  between operations: 14.2 us -> 0.67 us
    psum x2 -> x0, waiting for transfers between devices: 536 us -> none  [the longest x1 269 us: body(): whole_entry, whole_exit = lax.psum((right_entry, right_exit), 'dp')]
    all_gather x2 -> x0, blocking collectives: 165 us -> none  [the longest x1 92 us: body(): lax.all_gather(entry_start, 'dp', axis=0, tiled=True)]
    pallas_call x0 -> x2, Pallas kernels: none -> 98.8 us  [the longest x1 97.5 us: body(): pl.pallas_call(kernel, out_shape=jax.ShapeDtypeStruct((48, 32), F32), in_...]
    dot_general x18 -> x0, matrix products: 23.1 us -> none  [product(): jnp.dot(a, b, precision=lax.Precision.HIGHEST, preferred_element_type=jnp...]
    another operation x10 -> x0, other arithmetic: 13.4 us -> none  [the longest x6 7.19 us: orthonormal(): lower = jnp.linalg.cholesky(gram)]
  transfers between devices with their start and end apart: 2 -> 0, of which waited for: 2 -> 0; matrix products, arithmetic and copies ran while one was open for 0% -> 0% of each run, Pallas kernels for 0% -> 0%
where the time goes in v1:
time: 111 us; the launch traced here: 110 us
  Pallas kernels  98.8 us (89%)
  local copies, waits for them, and re-layouts  10.5 us (9%)
    pallas_call x1, Pallas kernels, body(): pl.pallas_call(kernel, out_shape=jax.ShapeDtypeStruct((48, 32), F32), in_...  97.5 us
    unnamed x22, local copies, waits for them, and re-layouts  10.5 us

profile of v1, /device:TPU:1, one launch (start us, length us, event | category | flops | bytes accessed | tf_op | source)
XLA Modules:
  0.0 110.0 jit_solution(10197005848192114185)
XLA Ops:
  0.6 0.0 copy-start
  0.6 1.4 %copy-done = bf16[128,6144]{1,0:T(8,128)(2,1)S(1)} copy-done((bf16[128,6144]{1,0:T(8,128)(2,1)S(1)}, bf16[128,6144]{1,0:T(8,128)(2,1)}, u32[]{:S(2)}) %copy-start) | copy-done | bytes 1572888
  2.0 0.0 copy-start.1
  2.0 1.2 %copy-done.1 = bf16[128,4096]{1,0:T(8,128)(2,1)S(1)} copy-done((bf16[128,4096]{1,0:T(8,128)(2,1)S(1)}, bf16[128,4096]{1,0:T(8,128)(2,1)}, u32[]{:S(2)}) %copy-start.1) | copy-done | bytes 1048600
  3.3 0.0 copy-start.2
  3.3 1.1 %copy-done.2 = bf16[128,3072]{1,0:T(8,128)(2,1)S(1)} copy-done((bf16[128,3072]{1,0:T(8,128)(2,1)S(1)}, bf16[128,3072]{1,0:T(8,128)(2,1)}, u32[]{:S(2)}) %copy-start.2) | copy-done | bytes 786456
  4.4 0.0 copy-start.3
  4.4 1.1 %copy-done.3 = bf16[128,3072]{1,0:T(8,128)(2,1)S(1)} copy-done((bf16[128,3072]{1,0:T(8,128)(2,1)S(1)}, bf16[128,3072]{1,0:T(8,128)(2,1)}, u32[]{:S(2)}) %copy-start.3) | copy-done | bytes 786456
  5.5 0.0 copy-start.4
  5.5 0.9 copy-done.4
  6.5 0.0 copy-start.5
  6.5 0.9 copy-done.5
  7.4 0.0 copy-start.7
  7.4 0.9 copy-done.7
  8.3 0.0 copy-start.8
  8.3 0.9 copy-done.8
  9.2 0.0 copy-start.9
  9.2 0.7 copy-done.9
  9.9 0.0 copy-start.10
  9.9 0.7 copy-done.10
  10.5 97.5 %powersgd.1.packed = f32[48,32]{1,0:T(8,128)S(1)} custom-call(bf16[128,3072]{1,0:T(8,128)(2,1)S(1)} %copy-done.2, bf16[128,6144]{1,0:T(8,128)(2,1)S(1)} %copy-done, bf16[128,4096]{1,0:T(8,128)(2,1)S(1)} %copy-done.1, bf16[128,3072]{1,0:T(8,128)(2,1)S(1)} %copy-done.3, bf16[16,3072]{1,0:T(8,128)(2,1)S(1)} %copy-done.7, bf16[16,6144]{1,0:T(8,128)(2,1)S(1)} %copy-done.4, ...), custom_call_target="tpu_custom_call" | custom-call | tf_op jit(solution)/shard_map/powersgd/pallas_call | solution.py:434
  108.0 0.0 copy-start.6
  108.0 0.6 copy-done.6
  108.6 1.3 %outputs.1 = (f32[6,32]{1,0:T(8,128)}, f32[8,32]{1,0:T(8,128)}, f32[12,32]{1,0:T(8,128)}, f32[6,32]{1,0:T(8,128)}) custom-call(f32[48,32]{1,0:T(8,128)} %copy-done.6), custom_call_target="tpu_custom_call" | custom-call | tf_op jit(solution)/shard_map/outputs/pallas_call | solution.py:445
Async XLA Ops:
  0.6 1.4 %copy-start = (bf16[128,6144]{1,0:T(8,128)(2,1)S(1)}, bf16[128,6144]{1,0:T(8,128)(2,1)}, u32[]{:S(2)}) copy-start(bf16[128,6144]{1,0:T(8,128)(2,1)} %entry_grad.1) | copy-start | bytes 4718596
  2.0 1.2 %copy-start.1 = (bf16[128,4096]{1,0:T(8,128)(2,1)S(1)}, bf16[128,4096]{1,0:T(8,128)(2,1)}, u32[]{:S(2)}) copy-start(bf16[128,4096]{1,0:T(8,128)(2,1)} %exit_input.1) | copy-start | bytes 3145732
  3.3 1.1 %copy-start.2 = (bf16[128,3072]{1,0:T(8,128)(2,1)S(1)}, bf16[128,3072]{1,0:T(8,128)(2,1)}, u32[]{:S(2)}) copy-start(bf16[128,3072]{1,0:T(8,128)(2,1)} %entry_input.1) | copy-start | bytes 2359300
  4.4 1.1 %copy-start.3 = (bf16[128,3072]{1,0:T(8,128)(2,1)S(1)}, bf16[128,3072]{1,0:T(8,128)(2,1)}, u32[]{:S(2)}) copy-start(bf16[128,3072]{1,0:T(8,128)(2,1)} %exit_grad.1) | copy-start | bytes 2359300
  5.5 0.9 copy-start.4
  6.5 0.9 copy-start.5
  7.4 0.9 copy-start.7
  8.3 0.9 copy-start.8
  9.2 0.7 copy-start.9
  9.9 0.7 copy-start.10
  108.0 0.6 copy-start.6

commit v2 on v0

v2 whole, which is shorter than its diff:
```python
import math

import jax
import jax.numpy as jnp
from jax import lax
from jax.experimental import pallas as pl
from jax.experimental.pallas import tpu as pltpu
from jax.sharding import PartitionSpec as P

MESH = pl.DeviceIdType.MESH
NY, NZ, NX = 8, 8, 4
GROUPS = 4
HALF = 4
FAR = (4, 3, 5, 2, 6, 1, 7)
FAR_X = (2, 1, 3)
TOK = 144
F32 = jnp.float32
BF16 = jnp.bfloat16
NT = (((1,), (1,)), ((), ()))
NN = (((1,), (0,)), ((), ()))
TN = (((0,), (0,)), ((), ()))


class Matrix:
    def __init__(self, width, outs, put_basis, put_factor):
        self.width, self.outs = width, outs
        self.nl, self.ns = width // (NY * 128), outs // (NY * 128)
        self.left_rows, self.right_rows = width // 512, outs // 512
        self.lanes = outs // (NY * NZ)
        self.put_basis, self.put_factor = put_basis, put_factor


ENTRY = Matrix(3072, 6144, 0, 16)
EXIT = Matrix(4096, 3072, 8, 32)


def device(y, z, x, c):
    return ((y * NZ + z) * NX + x) * 2 + c


def split3(v):
    hi = v.astype(BF16)
    rest = v - hi.astype(F32)
    mid = rest.astype(BF16)
    lo = (rest - mid.astype(F32)).astype(BF16)
    return jnp.concatenate([hi, mid, lo], axis=0)


def fold3(v):
    return v[0:32] + v[32:64] + v[64:96]


def exact_dot(a, b, dims):
    return lax.dot_general(a, b, dims, precision=lax.Precision.HIGHEST, preferred_element_type=F32)


def iota(shape, dim):
    return lax.broadcasted_iota(jnp.int32, shape, dim)


def kernel(
    entry_input, entry_grad, exit_input, exit_grad,
    entry_left, entry_right, exit_left, exit_right,
    entry_start, exit_start,
    out, load_sem, entry_scratch, exit_scratch,
):
    me = lax.axis_index("dp")
    y, z, x, c = me // (NZ * NX * 2), (me // (NX * 2)) % NZ, (me // 2) % NX, me % 2
    active_core = y // HALF
    active = c == active_core
    passive = c != active_core
    other = device(y, z, x, 1 - c)
    spot = 2 * x + c
    pair = (y // 2) % 2
    issued = [[]]

    def remote(src, dst, ss, rs, target):
        return pltpu.make_async_remote_copy(
            src_ref=src, dst_ref=dst, send_sem=ss, recv_sem=rs, device_id=(target,), device_id_type=MESH
        )

    def guarded(cond, fn):
        if cond is None:
            fn()
        else:
            @pl.when(cond)
            def _():
                fn()

    def send(copies, ss, moved, cond=None):
        def start():
            for src, dst, rs, target in copies:
                remote(src, dst, ss, rs, target).start()

        guarded(cond, start)
        issued[-1].append((cond, remote(moved, moved, ss, ss, other)))

    def arrive(dst, rs, cond=None):
        guarded(cond, remote(dst, dst, rs, rs, other).wait_recv)

    def drain(rounds):
        while len(issued) > rounds:
            for cond, copy in issued.pop(0):
                guarded(cond, copy.wait_send)

    barrier = pltpu.get_barrier_semaphore()
    peers = [device(y, z, (x + k // 2) % NX, (c + k) % 2) for k in range(1, 8)]
    peers += [device(y, (z + k) % NZ, x, c) for k in range(1, 8)]
    peers += [device((y + k) % NY, z, x, c) for k in range(1, 8)]
    for peer in peers:
        pl.semaphore_signal(barrier, inc=1, device_id=(peer,), device_id_type=MESH)

    loads = []
    for i, (src, dst, row, rows) in enumerate((
        (entry_grad, entry_scratch["wg"], 0, 128), (entry_right, entry_scratch["wg"], 128, 16),
        (exit_grad, exit_scratch["wg"], 0, 128), (exit_right, exit_scratch["wg"], 128, 16),
        (entry_input, entry_scratch["wx"], 0, 128), (entry_left, entry_scratch["wx"], 128, 16),
        (exit_input, exit_scratch["wx"], 0, 128), (exit_left, exit_scratch["wx"], 128, 16),
    )):
        copy = pltpu.make_async_copy(src, dst.at[pl.ds(row, rows)], load_sem.at[i])
        copy.start()
        loads.append(copy)

    def tiles(whole, first, count):
        return jnp.concatenate(
            [jnp.concatenate([whole[g, first + t] for t in range(count)], axis=1) for g in range(GROUPS)], axis=0
        )

    def columns(ref, slab, count):
        return ref[:, pl.ds(pl.multiple_of(slab * (128 * count), 128), 128 * count)]

    def contract(whole, n, weights, slab):
        pieces = split3(tiles(whole, slab * n, n))
        part = lax.dot_general(pieces, columns(weights, slab, n), NT, preferred_element_type=F32)
        return fold3(part), pieces

    def expand(pieces, weights, slab, n, whole):
        part = fold3(lax.dot_general(pieces, columns(weights, slab, n), NN, preferred_element_type=F32))
        for g in range(GROUPS):
            for t in range(n):
                whole[g, slab * n + t] = part[8 * g:8 * g + 8, 128 * t:128 * t + 128]

    def batches(half, far_first):
        near = jnp.where(half == active_core, pair, 1 - pair)
        first = 1 - near if far_first else near
        return [(b, HALF * half + 2 * b) for b in (first, 1 - first)]

    def gather(whole, n, sems, moved, use):
        ys, yr, xs, xr, cs, cr = sems

        def part(group, slab, count):
            return whole.at[group, pl.ds(slab * n, count * n)]

        def full(slab):
            return whole.at[:, pl.ds(slab * n, 2 * n)]

        mine = part(x, y, 1)
        send(
            [(mine, mine, yr.at[(y // 2) % 2], device((y + k) % NY, z, x, c)) for k in FAR],
            ys, moved.at[pl.ds(0, 7)], active,
        )
        yield
        for b, slab in batches(c, False):
            own = active & (b == pair)
            arrive(part(x, slab, 1), yr.at[b], own)
            arrive(part(x, slab, 2), yr.at[b], jnp.logical_not(own))
            both = part(x, slab, 2)
            send(
                [(both, both, xr.at[b], device(y, z, (x + k) % NX, c)) for k in FAR_X],
                xs.at[b], whole.at[pl.ds(0, 3), pl.ds(0, 2 * n)],
            )
        yield
        for b, slab in batches(c, False):
            arrive(whole.at[pl.ds(0, 3), pl.ds(0, 2 * n)], xr.at[b])
            send([(full(slab), full(slab), cr.at[b], other)], cs.at[b], full(slab))
        for b, slab in batches(c, False):
            use(slab)
            use(slab + 1)
        yield
        for b, slab in batches(1 - c, False):
            arrive(full(slab), cr.at[b])
            use(slab)
            use(slab + 1)

    def reduce(n, pieces, weights, buffers, sems):
        local, from_core, from_x, y_send, from_y = buffers
        cs, cr, xs, xr, ys, yr = sems
        for b, slab in batches(1 - c, True):
            expand(pieces, weights, slab, n, local)
            expand(pieces, weights, slab + 1, n, local)
            src = local.at[:, pl.ds(slab * n, 2 * n)]
            send([(src, from_core.at[:, pl.ds(2 * b * n, 2 * n)], cr.at[b], other)], cs.at[b], src)
        for b, slab in batches(c, True):
            expand(pieces, weights, slab, n, local)
            expand(pieces, weights, slab + 1, n, local)
        yield
        for b, slab in batches(c, True):
            arrive(from_core.at[:, pl.ds(2 * b * n, 2 * n)], cr.at[b])
            for g in range(GROUPS):
                for t in range(2 * n):
                    local[g, slab * n + t] = local[g, slab * n + t] + from_core[g, 2 * b * n + t]
            send(
                [
                    (
                        local.at[(x + k) % NX, pl.ds(slab * n, 2 * n)], from_x.at[x, pl.ds(2 * b * n, 2 * n)],
                        xr.at[b], device(y, z, (x + k) % NX, c),
                    )
                    for k in FAR_X
                ],
                xs.at[b], from_x.at[pl.ds(0, 3), pl.ds(0, 2 * n)],
            )
        yield
        for b, slab in batches(c, True):
            arrive(from_x.at[pl.ds(0, 3), pl.ds(0, 2 * n)], xr.at[b])
            for i in range(2):
                for t in range(n):
                    total = local[x, (slab + i) * n + t]
                    for k in range(1, 4):
                        total = total + from_x[(x + k) % NX, (2 * b + i) * n + t]
                    y_send[2 * b + i, t] = total
                copy = remote(
                    y_send.at[2 * b + i], from_y.at[y], ys, yr, device(slab + i, z, x, c)
                )
                guarded(slab + i != y, copy.start)
        issued[-1].append((active, remote(from_y.at[pl.ds(0, 3)], from_y.at[pl.ds(0, 3)], ys, ys, other)))
        issued[-1].append((passive, remote(from_y.at[pl.ds(0, 4)], from_y.at[pl.ds(0, 4)], ys, ys, other)))
        yield

    def summed_over_y(n, buffers, sems):
        y_send, from_y = buffers[3:]
        arrive(from_y.at[pl.ds(0, 7)], sems[5])
        total = [y_send[y % HALF, t] for t in range(n)]
        for k in range(1, 8):
            for t in range(n):
                total[t] = total[t] + from_y[(y + k) % NY, t]
        return total

    lane = iota((8, 128), 1)
    grams, inverse = {}, {}

    def chain(m, start, s, load_g, load_x):
        rows = m.right_rows
        s["own"][...] = jnp.zeros_like(s["own"])
        s["own"][0:rows, :] = start[...]
        at = m.lanes * z + rows * spot
        pick = jnp.where(
            (iota((16, 128), 1) == (at + iota((16, 128), 0)) % 128) & (iota((16, 128), 0) < rows), 1.0, 0.0
        ).astype(F32)
        placed = exact_dot(s["own"][...], pick, TN)
        for g in range(GROUPS):
            s["first_send"][g] = placed[8 * g:8 * g + 8, :]
        yield
        first_ss, first_rs = s["first_sems"]
        landing = s["first_recv"].at[spot]
        send([(s["first_send"].at[x], landing, first_rs, other)], first_ss.at[0], s["first_send"].at[0], passive)
        send(
            [
                (s["first_send"].at[(x + k) % NX], landing, first_rs, device(y, z, (x + k) % NX, active_core))
                for k in FAR_X
            ],
            first_ss.at[1], s["first_send"].at[pl.ds(0, 3)],
        )
        yield

        @pl.when(active)
        def _():
            arrive(s["first_recv"].at[pl.ds(0, 7)], first_rs)
            total = s["first_send"][x]
            for k in range(1, 8):
                total = total + s["first_recv"][(spot + k) % 8]
            s["zs_send"][...] = total

        zs_ss, zs_rs = s["zs_sems"]
        send(
            [(s["zs_send"], s["zs_recv"].at[z], zs_rs, device(y, (z + k) % NZ, x, c)) for k in FAR],
            zs_ss, s["zs_recv"].at[pl.ds(0, 7)], active,
        )
        yield

        @pl.when(active)
        def _():
            s["zs_recv"][z] = s["zs_send"][...]
            arrive(s["zs_recv"].at[pl.ds(0, 7)], zs_rs)
            slab = [jnp.zeros((8, 128), F32) for _ in range(m.ns)]
            for zz in range(NZ):
                t, first = divmod(m.lanes * zz, 128)
                piece = s["zs_recv"][zz]
                if first + m.lanes <= 128:
                    slab[t] = slab[t] + piece
                else:
                    slab[t] = slab[t] + jnp.where(lane >= first, piece, 0.0)
                    slab[t + 1] = slab[t + 1] + jnp.where(lane < first, piece, 0.0)
            for t in range(m.ns):
                s["s_all"][x, y * m.ns + t] = slab[t]

        for copy in load_g:
            copy.wait()
        total = [jnp.zeros((32, TOK), F32)]

        def use_start(slab):
            total[0] += contract(s["s_all"], m.ns, s["wg"], slab)[0]

        yield from gather(s["s_all"], m.ns, s["s_gather"], s["f_buffers"][4], use_start)
        left = split3(total[0])
        for copy in load_x:
            copy.wait()
        yield from reduce(m.nl, left, s["wx"], s["l_buffers"], s["l_reduce"])

        @pl.when(active)
        def _():
            total = summed_over_y(m.nl, s["l_buffers"], s["l_reduce"])
            for t in range(m.nl):
                s["l_zs"][t] = total[t]

        lz_ss, lz_rs = s["lz_sems"]
        send(
            [(s["l_zs"], s["l_z"].at[z], lz_rs, device(y, (z + k) % NZ, x, c)) for k in FAR],
            lz_ss, s["l_z"].at[pl.ds(0, 7)], active,
        )
        yield

        @pl.when(active)
        def _():
            for t in range(m.nl):
                s["l_z"][z, t] = s["l_zs"][t]
            arrive(s["l_z"].at[pl.ds(0, 7)], lz_rs)
            for t in range(m.nl):
                total = s["l_z"][0, t]
                for zz in range(1, NZ):
                    total = total + s["l_z"][zz, t]
                s["l_all"][x, y * m.nl + t] = total

        side = [jnp.zeros((32, TOK), F32), jnp.zeros((32, 96), F32)]

        def use_left(slab):
            part, pieces = contract(s["l_all"], m.nl, s["wx"], slab)
            side[0] += part
            side[1] += fold3(lax.dot_general(pieces, pieces, NT, preferred_element_type=F32))

        yield from gather(s["l_all"], m.nl, s["l_gather"], s["l_z"], use_left)
        grams[m] = side[1]
        right = split3(side[0])
        yield from reduce(m.ns, right, s["wg"], s["f_buffers"], s["f_reduce"])

        @pl.when(active)
        def _():
            total = summed_over_y(m.ns, s["f_buffers"], s["f_reduce"])
            for zz in range(NZ):
                t, first = divmod(m.lanes * zz, 128)
                if first + m.lanes <= 128:
                    s["f_zs"][zz] = total[t]
                else:
                    s["f_zs"][zz] = jnp.where(lane >= first, total[t], total[t + 1])

        fz_ss, fz_rs = s["fz_sems"]
        send(
            [(s["f_zs"].at[(z + k) % NZ], s["f_z"].at[z], fz_rs, device(y, (z + k) % NZ, x, c)) for k in FAR],
            fz_ss, s["f_z"].at[pl.ds(0, 7)], active,
        )
        yield

        @pl.when(active)
        def _():
            arrive(s["f_z"].at[pl.ds(0, 7)], fz_rs)
            total = s["f_zs"][z]
            for k in range(1, 8):
                total = total + s["f_z"][(z + k) % NZ]
            s["f_own"][...] = total

        last_ss, last_rs = s["last_sems"]
        send(
            [
                (s["f_own"], s["f_last"].at[x], last_rs, device(y, z, (x + k // 2) % NX, (c + k) % 2))
                for k in (4, 5, 2, 3, 6, 7, 1)
            ],
            last_ss, s["f_z"].at[pl.ds(0, 7)], active,
        )

        @pl.when(active)
        def _():
            s["f_last"][x] = s["f_own"][...]

        yield
        arrive(s["f_last"].at[pl.ds(0, 3)], last_rs, active)
        arrive(s["f_last"], last_rs, passive)
        raw = jnp.concatenate([s["f_last"][g] for g in range(GROUPS)], axis=0)
        own = exact_dot(pick, raw, NT)
        out[m.put_factor:m.put_factor + 16, :] = exact_dot(own, inverse[m], NT) * (1.0 / 512)

    def cholesky():
        row, column = iota((32, 32), 0), iota((32, 32), 1)
        rows = iota((32, 1), 0)
        state = {}
        for m in (ENTRY, EXIT):
            gram = grams[m]
            state[m] = [
                gram[:, 0:32] + gram[:, 32:64] + gram[:, 64:96],
                jnp.where(row == column, 1.0, 0.0).astype(F32),
                jnp.ones((32, 1), F32),
            ]
        for j in range(32):
            for m in (ENTRY, EXIT):
                left, unit, diagonal = state[m]
                pivot = left[j:j + 1, j:j + 1]
                factor = jnp.where(rows > j, left[:, j:j + 1] / pivot, 0.0)
                state[m] = [
                    left - factor * left[j:j + 1, :],
                    unit - factor * unit[j:j + 1, :],
                    jnp.where(rows == j, pivot, diagonal),
                ]
            if j % 11 == 10:
                yield
        for m, s in ((ENTRY, entry_scratch), (EXIT, exit_scratch)):
            inverse[m] = state[m][1] / jnp.sqrt(state[m][2])
            shape = (8, 128 * m.nl)
            at = m.left_rows * (8 * z + spot)
            pick = jnp.where(
                (iota(shape, 1) == at + iota(shape, 0)) & (iota(shape, 0) < m.left_rows), 1.0, 0.0
            ).astype(F32)
            own = exact_dot(pick, tiles(s["l_all"], y * m.nl, m.nl), NT)
            out[m.put_basis:m.put_basis + 8, :] = exact_dot(own, inverse[m], NT) * math.sqrt(m.width)
        yield

    chains = [
        chain(ENTRY, entry_start, entry_scratch, loads[0:2], loads[4:6]),
        chain(EXIT, exit_start, exit_scratch, loads[2:4], loads[6:8]),
    ]
    for step in chains:
        next(step)
    pl.semaphore_wait(barrier, len(peers))
    extra = None
    while chains:
        issued.append([])
        chains = [step for step in chains if next(step, chains) is None]
        drain(2)
        if extra is None and len(grams) == 2:
            extra = cholesky()
        elif extra is not None:
            next(extra, None)
    drain(0)


def outputs_kernel(packed, entry_basis, exit_basis, entry_factor, exit_factor):
    entry_basis[...] = packed[0:6, :]
    exit_basis[...] = packed[8:16, :]
    entry_factor[...] = packed[16:28, :]
    exit_factor[...] = packed[32:38, :]


def scratch_of(m):
    dma = pltpu.SemaphoreType.DMA

    def f32(*shape):
        return pltpu.VMEM(shape + (8, 128), F32)

    def gather_sems():
        return [dma, dma((2,)), dma((2,)), dma((2,)), dma((2,)), dma((2,))]

    def reduce_sems():
        return [dma((2,)), dma((2,)), dma((2,)), dma((2,)), dma, dma]

    def reduce_buffers(n):
        return [f32(4, 8 * n), f32(4, 4 * n), f32(4, 4 * n), f32(4, n), f32(8, n)]

    return {
        "wg": pltpu.VMEM((TOK, m.outs), BF16),
        "wx": pltpu.VMEM((TOK, m.width), BF16),
        "own": pltpu.VMEM((16, 32), F32),
        "first_send": f32(4), "first_recv": f32(8), "first_sems": [dma((2,)), dma],
        "zs_send": f32(), "zs_recv": f32(8), "zs_sems": [dma, dma],
        "s_all": f32(4, 8 * m.ns), "s_gather": gather_sems(),
        "l_buffers": reduce_buffers(m.nl), "l_reduce": reduce_sems(),
        "l_zs": f32(m.nl), "l_z": f32(8, m.nl), "lz_sems": [dma, dma],
        "l_all": f32(4, 8 * m.nl), "l_gather": gather_sems(),
        "f_buffers": reduce_buffers(m.ns), "f_reduce": reduce_sems(),
        "f_zs": f32(8), "f_z": f32(8), "fz_sems": [dma, dma],
        "f_own": f32(), "f_last": f32(4), "last_sems": [dma, dma],
    }


def body(*args):
    vmem = pl.BlockSpec(memory_space=pltpu.VMEM)
    hbm = pl.BlockSpec(memory_space=pltpu.HBM)
    packed = pl.pallas_call(
        kernel,
        out_shape=jax.ShapeDtypeStruct((48, 32), F32),
        in_specs=[hbm] * 8 + [vmem] * 2,
        out_specs=vmem,
        scratch_shapes=[pltpu.SemaphoreType.DMA((8,)), scratch_of(ENTRY), scratch_of(EXIT)],
        compiler_params=pltpu.CompilerParams(
            collective_id=0, has_side_effects=True, vmem_limit_bytes=63 * 1024 * 1024
        ),
        name="powersgd",
    )(*args)
    return pl.pallas_call(
        outputs_kernel,
        out_shape=tuple(jax.ShapeDtypeStruct((rows, 32), F32) for rows in (6, 8, 12, 6)),
        in_specs=[vmem],
        out_specs=(vmem,) * 4,
        name="outputs",
    )(packed)


def solution(mesh):
    spec = P("dp", None)
    return jax.shard_map(body, mesh=mesh, in_specs=(spec,) * 10, out_specs=(spec,) * 4, check_vma=False)
```

time: 765 us -> 92.7 us (0.12)
  waiting for transfers between devices: 536 us -> 0 us
  blocking collectives: 165 us -> 0 us
  Pallas kernels: 0 us -> 91.9 us
  matrix products: 25.2 us -> 0 us
  other arithmetic: 15.2 us -> 0 us
  between operations: 14.2 us -> 0.64 us
  local copies, waits for them, and re-layouts: 9.25 us -> 0 us
    psum x2 -> x0, waiting for transfers between devices: 536 us -> none  [the longest x1 269 us: body(): whole_entry, whole_exit = lax.psum((right_entry, right_exit), 'dp')]
    all_gather x2 -> x0, blocking collectives: 165 us -> none  [the longest x1 92 us: body(): lax.all_gather(entry_start, 'dp', axis=0, tiled=True)]
    pallas_call x0 -> x2, Pallas kernels: none -> 91.9 us  [the longest x1 90.5 us: body(): pl.pallas_call(kernel, out_shape=jax.ShapeDtypeStruct((48, 32), F32), in_...]
    dot_general x18 -> x0, matrix products: 23.1 us -> none  [product(): jnp.dot(a, b, precision=lax.Precision.HIGHEST, preferred_element_type=jnp...]
    another operation x10 -> x0, other arithmetic: 13.4 us -> none  [the longest x6 7.19 us: orthonormal(): lower = jnp.linalg.cholesky(gram)]
    unnamed x28 -> x0, local copies, waits for them, and re-layouts: 9.11 us -> none
  transfers between devices with their start and end apart: 2 -> 0, of which waited for: 2 -> 0; matrix products, arithmetic and copies ran while one was open for 0% -> 0% of each run, Pallas kernels for 0% -> 0%
where the time goes in v2:
time: 92.7 us; the launch traced here: 92.5 us
  Pallas kernels  91.9 us (99%)
    pallas_call x1, Pallas kernels, body(): pl.pallas_call(kernel, out_shape=jax.ShapeDtypeStruct((48, 32), F32), in_...  90.5 us

profile of v2, /device:TPU:1, one launch (start us, length us, event | category | flops | bytes accessed | tf_op | source)
XLA Modules:
  0.0 92.5 jit_solution(416275146871043022)
XLA Ops:
  0.6 90.5 %powersgd.1.packed = f32[48,32]{1,0:T(8,128)} custom-call(bf16[128,3072]{1,0:T(8,128)(2,1)} %entry_input.1, bf16[128,6144]{1,0:T(8,128)(2,1)} %entry_grad.1, bf16[128,4096]{1,0:T(8,128)(2,1)} %exit_input.1, bf16[128,3072]{1,0:T(8,128)(2,1)} %exit_grad.1, bf16[16,3072]{1,0:T(8,128)(2,1)} %entry_left.1, bf16[16,6144]{1,0:T(8,128)(2,1)} %entry_right.1, ...), custom_call_target="tpu_custom_call" | custom-call | tf_op jit(solution)/shard_map/powersgd/pallas_call | solution.py:484
  91.1 1.3 %outputs.1 = (f32[6,32]{1,0:T(8,128)}, f32[8,32]{1,0:T(8,128)}, f32[12,32]{1,0:T(8,128)}, f32[6,32]{1,0:T(8,128)}) custom-call(f32[48,32]{1,0:T(8,128)} %powersgd.1.packed), custom_call_target="tpu_custom_call" | custom-call | tf_op jit(solution)/shard_map/outputs/pallas_call | solution.py:495

commit v3 on v2

--- a/solution.py
+++ b/solution.py
@@ -110,6 +110,11 @@
     for peer in peers:
         pl.semaphore_signal(barrier, inc=1, device_id=(peer,), device_id_type=MESH)
 
+    starts = []
+    for i, (src, s) in enumerate(((entry_start, entry_scratch), (exit_start, exit_scratch))):
+        copy = pltpu.make_async_copy(src, s["start"], load_sem.at[8 + i])
+        copy.start()
+        starts.append(copy)
     loads = []
     for i, (src, dst, row, rows) in enumerate((
         (entry_grad, entry_scratch["wg"], 0, 128), (entry_right, entry_scratch["wg"], 128, 16),
@@ -176,7 +181,6 @@
         for b, slab in batches(c, False):
             use(slab)
             use(slab + 1)
-        yield
         for b, slab in batches(1 - c, False):
             arrive(full(slab), cr.at[b])
             use(slab)
@@ -193,7 +197,6 @@
         for b, slab in batches(c, True):
             expand(pieces, weights, slab, n, local)
             expand(pieces, weights, slab + 1, n, local)
-        yield
         for b, slab in batches(c, True):
             arrive(from_core.at[:, pl.ds(2 * b * n, 2 * n)], cr.at[b])
             for g in range(GROUPS):
@@ -241,7 +244,8 @@
     def chain(m, start, s, load_g, load_x):
         rows = m.right_rows
         s["own"][...] = jnp.zeros_like(s["own"])
-        s["own"][0:rows, :] = start[...]
+        start.wait()
+        s["own"][0:rows, :] = s["start"][...]
         at = m.lanes * z + rows * spot
         pick = jnp.where(
             (iota((16, 128), 1) == (at + iota((16, 128), 0)) % 128) & (iota((16, 128), 0) < rows), 1.0, 0.0
@@ -408,7 +412,7 @@
                     unit - factor * unit[j:j + 1, :],
                     jnp.where(rows == j, pivot, diagonal),
                 ]
-            if j % 11 == 10:
+            if j == 15:
                 yield
         for m, s in ((ENTRY, entry_scratch), (EXIT, exit_scratch)):
             inverse[m] = state[m][1] / jnp.sqrt(state[m][2])
@@ -422,8 +426,8 @@
         yield
 
     chains = [
-        chain(ENTRY, entry_start, entry_scratch, loads[0:2], loads[4:6]),
-        chain(EXIT, exit_start, exit_scratch, loads[2:4], loads[6:8]),
+        chain(ENTRY, starts[0], entry_scratch, loads[0:2], loads[4:6]),
+        chain(EXIT, starts[1], exit_scratch, loads[2:4], loads[6:8]),
     ]
     for step in chains:
         next(step)
@@ -435,7 +439,7 @@
         drain(2)
         if extra is None and len(grams) == 2:
             extra = cholesky()
-        elif extra is not None:
+        if extra is not None:
             next(extra, None)
     drain(0)
 
@@ -465,6 +469,7 @@
     return {
         "wg": pltpu.VMEM((TOK, m.outs), BF16),
         "wx": pltpu.VMEM((TOK, m.width), BF16),
+        "start": pltpu.VMEM((m.right_rows, 32), F32),
         "own": pltpu.VMEM((16, 32), F32),
         "first_send": f32(4), "first_recv": f32(8), "first_sems": [dma((2,)), dma],
         "zs_send": f32(), "zs_recv": f32(8), "zs_sems": [dma, dma],
@@ -484,9 +489,9 @@
     packed = pl.pallas_call(
         kernel,
         out_shape=jax.ShapeDtypeStruct((48, 32), F32),
-        in_specs=[hbm] * 8 + [vmem] * 2,
+        in_specs=[hbm] * 10,
         out_specs=vmem,
-        scratch_shapes=[pltpu.SemaphoreType.DMA((8,)), scratch_of(ENTRY), scratch_of(EXIT)],
+        scratch_shapes=[pltpu.SemaphoreType.DMA((10,)), scratch_of(ENTRY), scratch_of(EXIT)],
         compiler_params=pltpu.CompilerParams(
             collective_id=0, has_side_effects=True, vmem_limit_bytes=63 * 1024 * 1024
         ),

time: 92.7 us -> 87.5 us (0.944)
  Pallas kernels: 91.9 us -> 86.6 us
    pallas_call x1, Pallas kernels: 90.5 us -> 85.3 us  [body(): pl.pallas_call(kernel, out_shape=jax.ShapeDtypeStruct((48, 32), F32), in_...]
where the time goes in v3:
time: 87.5 us; the launch traced here: 87.3 us
  Pallas kernels  86.6 us (99%)
    pallas_call x1, Pallas kernels, body(): pl.pallas_call(kernel, out_shape=jax.ShapeDtypeStruct((48, 32), F32), in_...  85.3 us

profile of v3, /device:TPU:1, one launch (start us, length us, event | category | flops | bytes accessed | tf_op | source)
XLA Modules:
  0.0 87.3 jit_solution(18419773803111894183)
XLA Ops:
  0.6 85.3 %powersgd.1.packed = f32[48,32]{1,0:T(8,128)} custom-call(bf16[128,3072]{1,0:T(8,128)(2,1)} %entry_input.1, bf16[128,6144]{1,0:T(8,128)(2,1)} %entry_grad.1, bf16[128,4096]{1,0:T(8,128)(2,1)} %exit_input.1, bf16[128,3072]{1,0:T(8,128)(2,1)} %exit_grad.1, bf16[16,3072]{1,0:T(8,128)(2,1)} %entry_left.1, bf16[16,6144]{1,0:T(8,128)(2,1)} %entry_right.1, ...), custom_call_target="tpu_custom_call" | custom-call | tf_op jit(solution)/shard_map/powersgd/pallas_call | solution.py:489
  85.9 1.3 %outputs.1 = (f32[6,32]{1,0:T(8,128)}, f32[8,32]{1,0:T(8,128)}, f32[12,32]{1,0:T(8,128)}, f32[6,32]{1,0:T(8,128)}) custom-call(f32[48,32]{1,0:T(8,128)} %powersgd.1.packed), custom_call_target="tpu_custom_call" | custom-call | tf_op jit(solution)/shard_map/outputs/pallas_call | solution.py:500

commit v4 on v3

--- a/solution.py
+++ b/solution.py
@@ -104,9 +104,10 @@
                 guarded(cond, copy.wait_send)
 
     barrier = pltpu.get_barrier_semaphore()
-    peers = [device(y, z, (x + k // 2) % NX, (c + k) % 2) for k in range(1, 8)]
-    peers += [device(y, (z + k) % NZ, x, c) for k in range(1, 8)]
-    peers += [device((y + k) % NY, z, x, c) for k in range(1, 8)]
+    peers = []
+    for k in FAR:
+        peers += [device((y + k) % NY, z, x, c), device(y, (z + k) % NZ, x, c)]
+    peers += [device(y, z, (x + k // 2) % NX, (c + k) % 2) for k in (4, 5, 2, 3, 6, 7, 1)]
     for peer in peers:
         pl.semaphore_signal(barrier, inc=1, device_id=(peer,), device_id_type=MESH)
 
@@ -178,7 +179,6 @@
         for b, slab in batches(c, False):
             arrive(whole.at[pl.ds(0, 3), pl.ds(0, 2 * n)], xr.at[b])
             send([(full(slab), full(slab), cr.at[b], other)], cs.at[b], full(slab))
-        for b, slab in batches(c, False):
             use(slab)
             use(slab + 1)
         for b, slab in batches(1 - c, False):
@@ -189,15 +189,19 @@
     def reduce(n, pieces, weights, buffers, sems):
         local, from_core, from_x, y_send, from_y = buffers
         cs, cr, xs, xr, ys, yr = sems
-        for b, slab in batches(1 - c, True):
+        def give(b, slab):
             expand(pieces, weights, slab, n, local)
             expand(pieces, weights, slab + 1, n, local)
             src = local.at[:, pl.ds(slab * n, 2 * n)]
             send([(src, from_core.at[:, pl.ds(2 * b * n, 2 * n)], cr.at[b], other)], cs.at[b], src)
-        for b, slab in batches(c, True):
+
+        theirs, ours = batches(1 - c, True), batches(c, True)
+        give(*theirs[0])
+        for i, (b, slab) in enumerate(ours):
             expand(pieces, weights, slab, n, local)
             expand(pieces, weights, slab + 1, n, local)
-        for b, slab in batches(c, True):
+            if i == 0:
+                give(*theirs[1])
             arrive(from_core.at[:, pl.ds(2 * b * n, 2 * n)], cr.at[b])
             for g in range(GROUPS):
                 for t in range(2 * n):

time: 87.5 us -> 87.3 us (level)
  no operation moved by 1% of the time
where the time goes in v4:
time: 87.3 us; the launch traced here: 87.1 us
  Pallas kernels  86.5 us (99%)
    pallas_call x1, Pallas kernels, body(): pl.pallas_call(kernel, out_shape=jax.ShapeDtypeStruct((48, 32), F32), in_...  85.2 us

profile of v4, /device:TPU:1, one launch (start us, length us, event | category | flops | bytes accessed | tf_op | source)
XLA Modules:
  0.0 87.1 jit_solution(9501686199749228957)
XLA Ops:
  0.6 85.2 %powersgd.1.packed = f32[48,32]{1,0:T(8,128)} custom-call(bf16[128,3072]{1,0:T(8,128)(2,1)} %entry_input.1, bf16[128,6144]{1,0:T(8,128)(2,1)} %entry_grad.1, bf16[128,4096]{1,0:T(8,128)(2,1)} %exit_input.1, bf16[128,3072]{1,0:T(8,128)(2,1)} %exit_grad.1, bf16[16,3072]{1,0:T(8,128)(2,1)} %entry_left.1, bf16[16,6144]{1,0:T(8,128)(2,1)} %entry_right.1, ...), custom_call_target="tpu_custom_call" | custom-call | tf_op jit(solution)/shard_map/powersgd/pallas_call | solution.py:493
  85.8 1.3 %outputs.1 = (f32[6,32]{1,0:T(8,128)}, f32[8,32]{1,0:T(8,128)}, f32[12,32]{1,0:T(8,128)}, f32[6,32]{1,0:T(8,128)}) custom-call(f32[48,32]{1,0:T(8,128)} %powersgd.1.packed), custom_call_target="tpu_custom_call" | custom-call | tf_op jit(solution)/shard_map/outputs/pallas_call | solution.py:504
